TPU v7x, 32 devices: a whole 2x2x4 slice. The times are simulated.
32 devices in a mesh: groups: 2 (over y), shot: 4 (over z), freq: 4 (over x, core).
Axes of the slice: x: 2, y: 2, z: 4, core: 2. Of those that a mesh axis runs over, the one named last changes fastest.
Arguments:
- source_field: bfloat16 [4, 4096, 16, 2, 128], P('freq', ('groups', 'shot')), parts along dimension 1, may hold values from -6 to 6
- receiver_field: bfloat16 [4, 4096, 16, 2, 128], P('freq', ('groups', 'shot')), parts along dimension 1, may hold values from -6 to 6
- operator: bfloat16 [4, 32, 3, 2, 128, 128], P('freq', 'groups'), parts along dimension 1, may hold values from -0.21875 to 0.21875
- band_offsets: int32 [32, 3], P('groups'), parts along dimension 0, may hold values from -2 to 4, as said below
- survey_tiles: int32 [128, 2], P('groups'), parts along dimension 0, may hold values from 0 to 15, as said below
- survey_data: bfloat16 [4, 128, 2, 128, 128], P('freq', ('groups', 'shot')), parts along dimension 1, may hold values from -0.1875 to 0.1875
Outputs:
- image: float32 [2, 4096, 128], P(None, ('groups', 'shot', 'freq')), parts along dimension 1
There are 2 independent parts, one for each index of `groups`. A program takes and returns all parts, laid end to end along the dimension named above; each array names one. Nothing has to cross between parts.
Inputs may be any that keep to these rules, and one draw needn't show every extreme that they name: `band_offsets`: in each row the offsets rise strictly; band k of row block i acts on cell block (i + offset) mod 16. `survey_tiles`: tile t has source block t div (4), so each source block has 4 tiles; the receiver blocks of one source block's tiles differ.
All inputs are finite; a program needn't handle non-finite values.
Results may differ from a plain program's by a relative error of at most 0.005.
Values may be sent and summed in bfloat16 or wider, within the bound.
No kernel may reach another device: no remote copies, remote signals or barrier semaphores. Data moves between devices by JAX's collectives and lax.ppermute only.
A program may use at most 256 MiB of HBM per device.

v0:
```python
import math

import jax
import jax.numpy as jnp
from jax import lax
from jax.sharding import PartitionSpec as P

NR = 2048


def extrapolate(wavefield, operator, columns):
    row_count, blocks_x, components, block_size = wavefield.shape
    bands = columns.shape[1]
    real_part = operator[:, :, 0]
    imag_part = operator[:, :, 1]
    upper_rows = jnp.concatenate([real_part, imag_part], -1)
    lower_rows = jnp.concatenate([-imag_part, real_part], -1)
    real_block = jnp.concatenate([upper_rows, lower_rows], -2)
    real_block = real_block.reshape(blocks_x, bands, 2 * block_size, 2, block_size)
    chosen = jnp.take(wavefield, columns, axis=1).reshape(
        row_count, blocks_x, bands, 2 * block_size
    )
    result = jnp.einsum("sikc,ikcoy->soiy", chosen, real_block, preferred_element_type=jnp.float32)
    return result.astype(jnp.bfloat16)


def to_owners(wavefield, shot_count, own_cells):
    row_count = wavefield.shape[0]
    return wavefield.reshape(row_count, 2, shot_count, own_cells)


def to_tiles(wavefield, shot_count, own_cells):
    row_count, components, blocks_x, block_size = wavefield.shape
    if own_cells >= block_size:
        return to_owners(wavefield, shot_count, own_cells)
    factor = block_size // own_cells
    copies = jnp.broadcast_to(
        wavefield[:, :, :, None, :], (row_count, components, blocks_x, factor, block_size)
    )
    return copies.reshape(row_count, components, shot_count, block_size)


def data_product(source_cells, data_shard, survey_tiles, block_size, own_cells):
    source_count = source_cells.shape[0]
    receiver_blocks = NR // block_size
    blocks = source_cells.reshape(source_count // block_size, block_size, 2 * own_cells)
    block_ids = jnp.arange(receiver_blocks, dtype=jnp.int32)
    chosen = jnp.take(blocks, survey_tiles[:, 0], axis=0)
    products = jnp.einsum(
        "ncsr,nsk->ncrk",
        lax.all_gather(data_shard, "shot", axis=0, tiled=True),
        chosen,
        preferred_element_type=jnp.float32,
    )
    real_part = products[:, 0, :, :own_cells] - products[:, 1, :, own_cells:]
    imag_part = products[:, 0, :, own_cells:] + products[:, 1, :, :own_cells]
    contribution = jnp.concatenate([real_part, imag_part], -1)
    onehot = (survey_tiles[:, 1][:, None] == block_ids[None, :]).astype(jnp.float32)
    summed = jnp.einsum("nq,nrk->qrk", onehot, contribution, precision=lax.Precision.HIGHEST)
    return summed.reshape(NR, 2, own_cells).astype(jnp.bfloat16)


def image_tile(product, receiver_tile, block_size):
    row_count, components, own_cells = product.shape
    tiles_here = max(own_cells // block_size, 1)
    inner_cells = own_cells // tiles_here
    left = product.reshape(row_count, 2, tiles_here, inner_cells)
    right = receiver_tile.reshape(row_count, 2, tiles_here, block_size)
    turned = jnp.stack([-right[:, 1], right[:, 0]], 1)
    both = jnp.stack([right, turned], 1)
    result = jnp.einsum("rctx,rocty->otxy", left, both, preferred_element_type=jnp.float32)
    return result.reshape(2, own_cells, block_size)


def body(source_field, receiver_field, operator, band_offsets, survey_tiles, survey_data):
    shot_count = lax.axis_size("shot")
    freq_local = source_field.shape[0]
    blocks_x = source_field.shape[2]
    block_size = source_field.shape[4]
    own_cells = blocks_x * block_size // shot_count
    block_rows = jnp.arange(blocks_x, dtype=jnp.int32)[:, None]
    columns = (block_rows + band_offsets) % blocks_x
    source_next = extrapolate(source_field[0], operator[0], columns)
    receiver_next = extrapolate(receiver_field[0], operator[0], columns)
    source_send = to_owners(source_next, shot_count, own_cells)
    receiver_send = to_tiles(receiver_next, shot_count, own_cells)
    source_cells = lax.all_to_all(source_send, "shot", split_axis=2, concat_axis=0, tiled=True)
    receiver_tile = lax.all_to_all(receiver_send, "shot", split_axis=2, concat_axis=0, tiled=True)
    source_cells = source_cells.reshape(source_cells.shape[0], 2 * own_cells)
    product = data_product(source_cells, survey_data[0], survey_tiles, block_size, own_cells)
    receiver_tile = receiver_tile.reshape(receiver_tile.shape[0], 2, -1)
    image_sum = image_tile(product, receiver_tile, block_size)
    total_freqs = freq_local * lax.axis_size("freq")
    scaled = image_sum * (1.0 / math.sqrt(2.0 * NR * total_freqs))
    return lax.psum_scatter(scaled, "freq", scatter_dimension=1, tiled=True)


def solution(mesh):
    return jax.shard_map(
        body,
        mesh=mesh,
        in_specs=(
            P("freq", ("groups", "shot"), None, None, None),
            P("freq", ("groups", "shot"), None, None, None),
            P("freq", "groups", None, None, None, None),
            P("groups", None),
            P("groups", None),
            P("freq", ("groups", "shot"), None, None, None),
        ),
        out_specs=P(None, ("groups", "shot", "freq"), None),
        check_vma=False,
    )
```

profile of v0, /device:TPU:0, one launch (start us, length us, event | category | flops | bytes accessed | tf_op | source)
XLA Modules:
  0.0 638.6 jit_solution(4651620882753983201)
XLA Ops:
  6.5 3.5 copy.37
  13.6 36.4 %gather_fusion.1 = bf16[48,512,2,128]{3,2,1,0:T(2,128)(2,1)} fusion(bf16[512,16,2,128]{3,2,1,0:T(2,128)(2,1)} %bitcast.127, s32[1024]{0:T(1024)S(1)} %pad_clamp_fusion.1), kind=kCustom, calls=%fused_computation.clone | custom fusion | bytes 25166016 | tf_op jit(solution)/shard_map/jit(_take)/gather | solution.py:20
  50.0 36.4 %gather_fusion.2 = bf16[48,512,2,128]{3,2,1,0:T(2,128)(2,1)} fusion(bf16[512,16,2,128]{3,2,1,0:T(2,128)(2,1)} %bitcast.128, s32[1024]{0:T(1024)S(1)} %pad_clamp_fusion.1), kind=kCustom, calls=%fused_computation.1.clone | custom fusion | bytes 25166016 | tf_op jit(solution)/shard_map/jit(_take)/gather | solution.py:20
  86.4 26.5 %fusion.7 = (bf16[512,16,3,2,128]{4,3,0,2,1:T(2,128)(2,1)}, bf16[512,16,3,2,128]{4,3,0,2,1:T(2,128)(2,1)}) fusion(bf16[16,3,512,2,128]{4,3,2,1,0:T(2,128)(2,1)} %bitcast.126, pred[16,3]{1,0:T(8,128)(4,1)S(1)} %copy.38, bf16[16,3,512,2,128]{4,3,2,1,0:T(2,128)(2,1)} %bitcast.125), kind=kLoop, calls=%fused_computation.17 | loop fusion | flops 12582912 | bytes 50331696 | tf_op jit(solution)/shard_map/jit(_take)/select_n | solution.py:20
  112.9 20.8 %reshape.79 = bf16[512,16,3,256,1]{3,0,2,1,4:T(8,128)(2,1)} reshape(bf16[512,16,3,2,128]{4,3,0,2,1:T(2,128)(2,1)} %get-tuple-element.13) | data formatting | bytes 25165824 | tf_op jit(solution)/shard_map/reshape | solution.py:20
  133.7 5.1 maximum_maximum_fusion
  138.8 15.2 %fusion.18 = bf16[512,2,16,128]{0,3,1,2:T(8,128)(2,1)} fusion(bf16[16,3,256,2,128]{2,4,3,1,0:T(8,128)(2,1)} %bitcast.133, bf16[512,16,3,256,1]{3,0,2,1,4:T(8,128)(2,1)} %reshape.79), kind=kOutput, calls=%fused_computation.31 | convolution fusion | flops 3223322624 | bytes 23068672 | tf_op jit(solution)/shard_map/sikc,ikcoy->soiy/dot_general | solution.py:23
  154.1 2.6 copy.41
  156.7 2.5 copy.42
  159.2 6.3 all-to-all-start
  165.5 20.6 %reshape.81 = bf16[512,16,3,256,1]{3,0,2,1,4:T(8,128)(2,1)} reshape(bf16[512,16,3,2,128]{4,3,0,2,1:T(2,128)(2,1)} %get-tuple-element.12) | data formatting | bytes 25165824 | tf_op jit(solution)/shard_map/reshape | solution.py:20
  186.1 15.2 %fusion.17 = bf16[512,2,16,128]{0,3,1,2:T(8,128)(2,1)} fusion(bf16[16,3,256,2,128]{2,4,3,1,0:T(8,128)(2,1)} %bitcast.134, bf16[512,16,3,256,1]{3,0,2,1,4:T(8,128)(2,1)} %reshape.81), kind=kOutput, calls=%fused_computation.30 | convolution fusion | flops 3223322624 | bytes 23068672 | tf_op jit(solution)/shard_map/sikc,ikcoy->soiy/dot_general | solution.py:23
  201.3 2.6 copy.51
  206.4 52.7 %all-to-all-done = bf16[512,2,4,512]{0,3,1,2:T(8,128)(2,1)} async-done(((bf16[512,2,4,512]{0,3,1,2:T(8,128)(2,1)}), bf16[512,2,4,512]{0,3,1,2:T(8,128)(2,1)}, u32[]{:S(2)}, u32[]{:S(2)}) %all-to-all-start) | async-done | bytes 4194336 | tf_op jit(solution)/shard_map/all_to_all | solution.py:88
  259.1 4.9 all-to-all-start.1
  264.8 7.3 %copy.43 = bf16[4,512,2,1,512]{4,1,0,2,3:T(8,128)(2,1)} copy(bf16[4,512,2,1,512]{1,4,2,0,3:T(8,128)(2,1)} %bitcast.13) | data formatting | bytes 8388608 | tf_op jit(solution)/shard_map/all_to_all | solution.py:88
  272.1 7.1 %reshape_reshape.6 = bf16[2048,2,4,128]{3,2,0,1:T(4,128)(2,1)} reshape(bf16[4,512,2,1,512]{4,1,0,2,3:T(8,128)(2,1)} %copy.43) | data formatting | bytes 8388608 | tf_op jit(solution)/shard_map/reshape;reshape | solution.py:68
  279.2 6.9 %stack_reshape_reshape.3 = bf16[2048,1,2,4,128]{4,3,0,2,1:T(4,128)(2,1)} reshape(bf16[4,512,2,1,512]{4,1,0,2,3:T(8,128)(2,1)} %copy.43) | data formatting | bytes 8388608 | tf_op jit(solution)/shard_map/stack;reshape;reshape | solution.py:70
  286.1 138.0 %all-to-all-done.1 = bf16[512,2,4,512]{0,3,1,2:T(8,128)(2,1)} async-done(((bf16[512,2,4,512]{0,3,1,2:T(8,128)(2,1)}), bf16[512,2,4,512]{0,3,1,2:T(8,128)(2,1)}, u32[]{:S(2)}, u32[]{:S(2)}) %all-to-all-start.1) | async-done | bytes 4194336 | tf_op jit(solution)/shard_map/all_to_all | solution.py:87
  424.2 11.2 %copy.53 = bf16[4,512,2,1,512]{4,2,1,0,3:T(2,128)(2,1)} copy(bf16[4,512,2,1,512]{1,4,2,0,3:T(8,128)(2,1)} %bitcast.28) | data formatting | bytes 8388608 | tf_op jit(solution)/shard_map/all_to_all | solution.py:87
  435.4 7.7 %reshape_reshape.7 = bf16[16,128,1024]{2,1,0:T(8,128)(2,1)} reshape(bf16[4,512,2,1,512]{4,2,1,0,3:T(2,128)(2,1)} %copy.53) | data formatting | bytes 8388608 | tf_op jit(solution)/shard_map/reshape;reshape | solution.py:46
  443.0 10.0 %gather_fusion = bf16[64,128,1024]{2,1,0:T(8,128)(2,1)} fusion(bf16[16,128,1024]{2,1,0:T(8,128)(2,1)} %reshape_reshape.7, s32[1024]{0:T(1024)S(1)} %pad_clamp_fusion), kind=kCustom, calls=%fused_computation.2 | custom fusion | bytes 33554688 | tf_op jit(solution)/shard_map/jit(_take)/gather | solution.py:48
  453.0 32.3 %convolution_bitcast_fusion = f32[64,2,128,1024]{2,3,1,0:T(8,128)} fusion(bf16[64,128,1024]{2,1,0:T(8,128)(2,1)} %gather_fusion, pred[64]{0:T(512)(128)(4,1)S(1)} %and_bitcast_fusion, bf16[1,64,2,128,128]{4,3,2,0,1:T(8,128)(2,1)} %all-gather.3.cloned.1.call-done), kind=kOutput, calls=%fused_computation.4 | convolution fusion | flops 4303355904 | bytes 88080448 | tf_op jit(solution)/shard_map/ncsr,nsk->ncrk/dot_general | solution.py:49
  485.3 11.3 %fusion = f32[64,128,512]{1,2,0:T(8,128)S(1)} fusion(f32[64,2,128,1024]{2,3,1,0:T(8,128)} %convolution_bitcast_fusion), kind=kLoop, calls=%fused_computation.8 | loop fusion | flops 4194304 | bytes 50331648 | tf_op jit(solution)/shard_map/add | solution.py:56
  496.6 18.0 %fusion.2 = f32[64,128,512]{1,2,0:T(8,128)} fusion(f32[64,2,128,1024]{2,3,1,0:T(8,128)} %convolution_bitcast_fusion), kind=kLoop, calls=%fused_computation.11 | loop fusion | flops 4194304 | bytes 50331648 | tf_op jit(solution)/shard_map/sub | solution.py:55
  514.7 2.8 copy.47
  521.8 18.2 %pad_maximum_fusion = f32[64,128,1024]{1,2,0:T(8,128)} fusion(f32[64,128,512]{1,2,0:T(8,128)S(1)} %fusion, f32[64,128,512]{1,2,0:T(8,128)} %fusion.2), kind=kLoop, calls=%fused_computation.3 | loop fusion | flops 8388608 | bytes 67108864 | tf_op jit(solution)/shard_map/concatenate | solution.py:57
  540.0 32.1 %copy.58 = f32[64,128,1024]{2,0,1:T(8,128)} copy(f32[64,128,1024]{1,2,0:T(8,128)} %pad_maximum_fusion) | data formatting | bytes 67108864 | tf_op jit(solution)/shard_map/concatenate | solution.py:57
  572.1 17.6 %convolution_convert_fusion = bf16[16,128,1024]{2,0,1:T(8,128)(2,1)} fusion(f32[64,128,1024]{2,0,1:T(8,128)} %copy.58, s32[64]{0:T(128)S(1)} %get-tuple-element.14), kind=kOutput, calls=%fused_computation.35 | convolution fusion | flops 1612710912 | bytes 37748992 | tf_op jit(solution)/shard_map/nq,nrk->qrk/dot_general | solution.py:59
  589.7 7.4 %copy.59 = bf16[16,128,1024]{1,0,2:T(8,128)(2,1)} copy(bf16[16,128,1024]{2,0,1:T(8,128)(2,1)} %convolution_convert_fusion) | data formatting | bytes 8388608 | tf_op jit(solution)/shard_map/convert_element_type | solution.py:60
  597.0 7.3 %convert_element_type.25 = bf16[2048,2,4,128]{0,3,2,1:T(8,128)(2,1)} reshape(bf16[16,128,1024]{1,0,2:T(8,128)(2,1)} %copy.59) | data formatting | bytes 8388608 | tf_op jit(solution)/shard_map/convert_element_type | solution.py:60
  611.1 20.6 %reduce-scatter.2.cloned.1.call-done = f32[2,128,128]{2,1,0:T(8,128)} async-done(((f32[2,512,128]{2,1,0:T(8,128)}), f32[2,128,128]{2,1,0:T(8,128)}) %reduce-scatter.2.cloned.1.call-update) | async-done | bytes 131088 | tf_op jit(solution)/shard_map/reduce_scatter | solution.py:95
  (38 shorter events, 17.9 us)
Async XLA Ops:
  10.0 3.3 copy-start.6
  112.9 20.8 %copy-start.2 = (bf16[16,3,128,128]{2,3,1,0:T(8,128)(2,1)S(1)}, bf16[16,3,128,128]{2,3,1,0:T(8,128)(2,1)}, u32[]{:S(2)}) copy-start(bf16[16,3,128,128]{2,3,1,0:T(8,128)(2,1)} %fusion.47) | copy-start | bytes 4718596
  112.9 20.8 %copy-start.3 = (bf16[16,3,128,128]{2,3,1,0:T(8,128)(2,1)S(1)}, bf16[16,3,128,128]{2,3,1,0:T(8,128)(2,1)}, u32[]{:S(2)}) copy-start(bf16[16,3,128,128]{2,3,1,0:T(8,128)(2,1)} %get-tuple-element.10) | copy-start | bytes 4718596
  159.2 100.0 %all-to-all-start = ((bf16[512,2,4,512]{0,3,1,2:T(8,128)(2,1)}), bf16[512,2,4,512]{0,3,1,2:T(8,128)(2,1)}, u32[]{:S(2)}, u32[]{:S(2)}) async-start(bf16[512,2,4,512]{0,3,1,2:T(8,128)(2,1)} %copy.42), calls=%async_computation | async-start | bytes 8388608 | tf_op jit(solution)/shard_map/all_to_all | solution.py:88
  206.4 58.4 %copy-start.7 = (s32[64,2]{0,1:T(2,128)S(1)}, s32[64,2]{0,1:T(2,128)}, u32[]{:S(2)}) copy-start(s32[64,2]{0,1:T(2,128)} %param.12) | copy-start | bytes 1540
  259.1 165.0 %all-to-all-start.1 = ((bf16[512,2,4,512]{0,3,1,2:T(8,128)(2,1)}), bf16[512,2,4,512]{0,3,1,2:T(8,128)(2,1)}, u32[]{:S(2)}, u32[]{:S(2)}) async-start(bf16[512,2,4,512]{0,3,1,2:T(8,128)(2,1)} %copy.52), calls=%async_computation.1 | async-start | bytes 8388608 | tf_op jit(solution)/shard_map/all_to_all | solution.py:87
  264.0 189.0 %all-gather.3.cloned.1.call-start = ((), (), s32[]{:S(2)}) async-start(), calls=%async_computation.4 | async-start | bytes 5242880 | tf_op jit(solution)/shard_map/all_gather | solution.py:51
  264.7 367.0 %reduce-scatter.2.cloned.1.call-start = ((), (), s32[]{:S(2)}) async-start(), calls=%async_computation.3 | async-start | bytes 655360 | tf_op jit(solution)/shard_map/reduce_scatter | solution.py:95
  496.6 18.0 %copy-start.1 = (bf16[2048,1,2,4,128]{4,3,0,2,1:T(4,128)(2,1)S(1)}, bf16[2048,1,2,4,128]{4,3,0,2,1:T(4,128)(2,1)}, u32[]{:S(2)}) copy-start(bf16[2048,1,2,4,128]{4,3,0,2,1:T(4,128)(2,1)} %stack_reshape_reshape.3) | copy-start | bytes 12582916
  514.7 3.6 copy-start
  604.3 2.8 copy-start.4
  604.3 4.1 copy-start.5
Sparse Core Ops, SparseCore 0:
  266.4 147.7 all-gather.2
  611.2 20.4 reduce-scatter.1
where the time goes:
time: 642 us; the launch traced here: 639 us
  local copies, waits for them, and re-layouts  236 us (37%)
  waiting for transfers between devices  212 us (33%)
  other arithmetic  83.2 us (13%)
  matrix products  82.1 us (13%)
  between operations  13.6 us (2%)
  starting transfers between devices  11.3 us (2%)
    all_to_all x1, waiting for transfers between devices, body(): lax.all_to_all(source_send, 'shot', split_axis=2, concat_axis=0, tiled=True)  138 us
    gather x2, local copies, waits for them, and re-layouts, extrapolate(): jnp.take(wavefield, columns, axis=1)  72.8 us
    all_to_all x1, waiting for transfers between devices, body(): lax.all_to_all(receiver_send, 'shot', split_axis=2, concat_axis=0, tiled=...  52.7 us
    reshape x2, local copies, waits for them, and re-layouts, extrapolate(): jnp.take(wavefield, columns, axis=1)  41.4 us
    dot_general x1, matrix products, data_product(): jnp.einsum('ncsr,nsk->ncrk', lax.all_gather(data_shard, 'shot', axis=0, t...  32.3 us
    concatenate x1, local copies, waits for them, and re-layouts, data_product(): contribution = jnp.concatenate([real_part, imag_part], -1)  32.1 us
    dot_general x2, matrix products, extrapolate(): jnp.einsum('sikc,ikcoy->soiy', chosen, real_block, preferred_element_type...  30.5 us
    select_n x1, other arithmetic, extrapolate(): jnp.take(wavefield, columns, axis=1)  26.5 us
  transfers between devices with their start and end apart: 4, of which 3 were waited for; matrix products, arithmetic and copies ran while one was open for 14% of the time, Pallas kernels for 0%

commit v1 on v0

--- a/solution.py
+++ b/solution.py
@@ -1,11 +1,15 @@
+import functools
 import math
 
 import jax
 import jax.numpy as jnp
 from jax import lax
+from jax.experimental import pallas as pl
+from jax.experimental.pallas import tpu as pltpu
 from jax.sharding import PartitionSpec as P
 
 NR = 2048
+LIMIT = 48 * 1024 * 1024
 
 
 def extrapolate(wavefield, operator, columns):
@@ -72,7 +76,7 @@
     return result.reshape(2, own_cells, block_size)
 
 
-def body(source_field, receiver_field, operator, band_offsets, survey_tiles, survey_data):
+def general_body(source_field, receiver_field, operator, band_offsets, survey_tiles, survey_data):
     shot_count = lax.axis_size("shot")
     freq_local = source_field.shape[0]
     blocks_x = source_field.shape[2]
@@ -95,6 +99,248 @@
     return lax.psum_scatter(scaled, "freq", scatter_dimension=1, tiled=True)
 
 
+def params():
+    return pltpu.CompilerParams(vmem_limit_bytes=LIMIT)
+
+
+def extrapolate_kernel(order, columns, field, operator, first, second, stage, apart, *, rows, blocks, chunk):
+    step = pl.program_id(0)
+    lines = 2 * blocks
+    half = blocks // 2
+
+    @pl.when(step == 0)
+    def _():
+        def split(n, carry):
+            start = pl.multiple_of(n * (chunk * lines), chunk * lines)
+            stage[...] = field[pl.ds(start, chunk * lines), :].astype(jnp.float32)
+            to = pl.ds(pl.multiple_of(n * chunk, chunk), chunk)
+            for block in range(blocks):
+                for part in range(2):
+                    picked = stage[pl.ds(2 * block + part, chunk, stride=lines), :]
+                    apart[block, to, part * 128:(part + 1) * 128] = picked.astype(jnp.bfloat16)
+            return carry
+
+        lax.fori_loop(0, rows // chunk, split, 0)
+
+    block = order[step]
+    inputs = []
+    weights = []
+    for band in range(operator.shape[1]):
+        inputs.append(apart[columns[block, band]])
+        real = operator[0, band, 0]
+        imag = operator[0, band, 1]
+        weights.append(jnp.concatenate([real, imag], 1))
+        weights.append(jnp.concatenate([-imag, real], 1))
+    result = jnp.dot(
+        jnp.concatenate(inputs, 1), jnp.concatenate(weights, 0), preferred_element_type=jnp.float32
+    ).astype(jnp.bfloat16)
+
+    @pl.when(step < half)
+    def _():
+        first[0] = result
+
+    @pl.when(step >= half)
+    def _():
+        second[0] = result
+
+
+def extrapolate_blocks(field, operator, columns, order):
+    rows, blocks, _, size = field.shape
+    half = blocks // 2
+    bands = columns.shape[1]
+    chunk = 32
+    flat = field.reshape(rows * blocks * 2, size)
+    out = jax.ShapeDtypeStruct((half, rows, 2 * size), jnp.bfloat16)
+    return pl.pallas_call(
+        functools.partial(extrapolate_kernel, rows=rows, blocks=blocks, chunk=chunk),
+        grid_spec=pltpu.PrefetchScalarGridSpec(
+            num_scalar_prefetch=2,
+            grid=(blocks,),
+            in_specs=[
+                pl.BlockSpec((rows * blocks * 2, size), lambda j, o, c: (0, 0)),
+                pl.BlockSpec((1, bands, 2, size, size), lambda j, o, c: (o[j], 0, 0, 0, 0)),
+            ],
+            out_specs=[
+                pl.BlockSpec((1, rows, 2 * size), lambda j, o, c: (jnp.minimum(j, half - 1), 0, 0)),
+                pl.BlockSpec((1, rows, 2 * size), lambda j, o, c: (jnp.maximum(j - half, 0), 0, 0)),
+            ],
+            scratch_shapes=[
+                pltpu.VMEM((chunk * blocks * 2, size), jnp.float32),
+                pltpu.VMEM((blocks, rows, 2 * size), jnp.bfloat16),
+            ],
+        ),
+        out_shape=[out, out],
+        compiler_params=params(),
+        cost_estimate=pl.CostEstimate(
+            flops=2 * rows * blocks * bands * 4 * size * size,
+            bytes_accessed=16 * 1024 * 1024,
+            transcendentals=0,
+        ),
+        name="extrapolate",
+    )(order, columns, flat, operator)
+
+
+def product_kernel(near_ids, far_ids, near, far, near_data, far_data, out, turned, total):
+    size = near_data.shape[2]
+    tiles = near_data.shape[0]
+    sources = near.shape[1] // size
+    per_source = tiles // sources
+
+    @pl.when(pl.program_id(0) == 0)
+    def _():
+        for side, data in enumerate((near_data, far_data)):
+            for tile in range(tiles):
+                for part in range(2):
+                    turned[side * tiles + tile, :, part * size:(part + 1) * size] = data[tile, part].T
+
+    total[...] = jnp.zeros_like(total)
+    for side, (field, ids) in enumerate(((near, near_ids), (far, far_ids))):
+        for source in range(sources):
+            upper = field[0, source * size:(source + 1) * size, :]
+            lower = jnp.concatenate([-upper[:, size:], upper[:, :size]], 1)
+            both = jnp.concatenate([upper, lower], 0)
+            first = side * tiles + source * per_source
+            left = turned[first:first + per_source].reshape(per_source * size, 2 * size)
+            result = jnp.dot(left, both, preferred_element_type=jnp.float32)
+            for tile in range(per_source):
+                total[ids[source * per_source + tile]] += result[tile * size:(tile + 1) * size]
+    for block in range(total.shape[0]):
+        out[0, :, block * size:(block + 1) * size] = total[block].T.astype(jnp.bfloat16)
+
+
+def product_blocks(near, far, near_data, far_data, near_ids, far_ids):
+    blocks, rows, width = near.shape
+    tiles, _, size, _ = near_data.shape
+    receivers = NR // size
+    field_spec = pl.BlockSpec((1, rows, width), lambda j, a, b: (j, 0, 0))
+    data_spec = pl.BlockSpec(near_data.shape, lambda j, a, b: (0, 0, 0, 0))
+    return pl.pallas_call(
+        product_kernel,
+        grid_spec=pltpu.PrefetchScalarGridSpec(
+            num_scalar_prefetch=2,
+            grid=(blocks,),
+            in_specs=[field_spec, field_spec, data_spec, data_spec],
+            out_specs=pl.BlockSpec((1, width, NR), lambda j, a, b: (j, 0, 0)),
+            scratch_shapes=[
+                pltpu.VMEM((2 * tiles, size, width), jnp.bfloat16),
+                pltpu.VMEM((receivers, size, width), jnp.float32),
+            ],
+        ),
+        out_shape=jax.ShapeDtypeStruct((blocks, width, NR), jnp.bfloat16),
+        compiler_params=params(),
+        cost_estimate=pl.CostEstimate(
+            flops=2 * blocks * 2 * tiles * size * width * width,
+            bytes_accessed=16 * 1024 * 1024,
+            transcendentals=0,
+        ),
+        name="product",
+    )(near_ids, far_ids, near, far, near_data, far_data)
+
+
+def image_kernel(origin, product, field, before, out, *, size):
+    both = jnp.dot(product[0], field[0], preferred_element_type=jnp.float32)
+    out[0, 0] = before[0, 0] + both[:size, :size] + both[size:, size:]
+    out[0, 1] = before[0, 1] + both[size:, :size] - both[:size, size:]
+
+
+def first_image_kernel(origin, product, field, out, *, size):
+    both = jnp.dot(product[0], field[0], preferred_element_type=jnp.float32)
+    out[0, 0] = both[:size, :size] + both[size:, size:]
+    out[0, 1] = both[size:, :size] - both[:size, size:]
+
+
+def image_blocks(product, field, origin, before=None):
+    blocks, rows, width = field.shape
+    size = width // 2
+    image_spec = pl.BlockSpec((1, 2, size, size), lambda j, o: (j, 0, 0, 0))
+    specs = [
+        pl.BlockSpec((1, width, rows), lambda j, o: (j, 0, o[0])),
+        pl.BlockSpec((1, rows, width), lambda j, o: (j, 0, 0)),
+    ]
+    values = [product, field]
+    kernel = first_image_kernel
+    if before is not None:
+        specs.append(image_spec)
+        values.append(before)
+        kernel = image_kernel
+    return pl.pallas_call(
+        functools.partial(kernel, size=size),
+        grid_spec=pltpu.PrefetchScalarGridSpec(
+            num_scalar_prefetch=1, grid=(blocks,), in_specs=specs, out_specs=image_spec
+        ),
+        out_shape=jax.ShapeDtypeStruct((blocks, 2, size, size), jnp.float32),
+        compiler_params=params(),
+        cost_estimate=pl.CostEstimate(
+            flops=2 * blocks * rows * width * width,
+            bytes_accessed=6 * 1024 * 1024,
+            transcendentals=0,
+        ),
+        name="image",
+    )(origin, *values)
+
+
+def exchange(value, axis, bit):
+    count = lax.axis_size(axis)
+    return lax.ppermute(value, axis, [(i, i ^ bit) for i in range(count)])
+
+
+def keep_and_send(value, bit):
+    keep = lax.dynamic_index_in_dim(value, bit, 0, keepdims=False)
+    send = lax.dynamic_index_in_dim(value, 1 - bit, 0, keepdims=False)
+    return keep, send
+
+
+def split_body(source_field, receiver_field, operator, band_offsets, survey_tiles, survey_data):
+    blocks = source_field.shape[2]
+    size = source_field.shape[4]
+    tiles = survey_data.shape[1]
+    shot = lax.axis_index("shot")
+    freq = lax.axis_index("freq")
+    place = shot % 2
+    per_owner = blocks // lax.axis_size("shot")
+    steps = jnp.arange(blocks // 2, dtype=jnp.int32)
+    own = steps % per_owner + per_owner * (2 * (steps // per_owner) + place)
+    other = steps % per_owner + per_owner * (2 * (steps // per_owner) + 1 - place)
+    order = jnp.concatenate([own, other])
+    columns = (jnp.arange(blocks, dtype=jnp.int32)[:, None] + band_offsets) % blocks
+
+    far_data = exchange(survey_data[0], "shot", 1)
+    receiver_own, receiver_other = extrapolate_blocks(receiver_field[0], operator[0], columns, order)
+    receiver_3 = exchange(receiver_other, "shot", 3)
+    receiver_2 = exchange(receiver_own, "shot", 2)
+    source_own, source_other = extrapolate_blocks(source_field[0], operator[0], columns, order)
+    source_far = exchange(source_other, "shot", 1)
+    receiver_1 = exchange(receiver_other, "shot", 1)
+
+    ids = survey_tiles[:, 1]
+    near_ids = lax.dynamic_slice_in_dim(ids, shot * tiles, tiles)
+    far_ids = lax.dynamic_slice_in_dim(ids, (shot ^ 1) * tiles, tiles)
+    product = product_blocks(source_own, source_far, survey_data[0], far_data, near_ids, far_ids)
+    image = image_blocks(product, receiver_own, shot[None])
+    image = image_blocks(product, receiver_1, (shot ^ 1)[None], image)
+    image = image_blocks(product, receiver_2, (shot ^ 2)[None], image)
+    image = image_blocks(product, receiver_3, (shot ^ 3)[None], image)
+
+    image = image.reshape(2, 2, 2, 2, size, size)
+    keep, send = keep_and_send(image.transpose(2, 0, 1, 3, 4, 5), freq % 2)
+    image = keep + exchange(send, "freq", 1)
+    keep, send = keep_and_send(image.transpose(1, 0, 2, 3, 4), freq // 2)
+    image = keep + exchange(send, "freq", 2)
+    keep, send = keep_and_send(image, shot // 2)
+    image = keep + exchange(send, "shot", 2)
+    total_freqs = source_field.shape[0] * lax.axis_size("freq")
+    return image * (1.0 / math.sqrt(2.0 * NR * total_freqs))
+
+
+def body(source_field, *rest):
+    fits = (
+        lax.axis_size("shot") == 4
+        and lax.axis_size("freq") == 4
+        and source_field.shape[1:] == (512, 16, 2, 128)
+    )
+    return (split_body if fits else general_body)(source_field, *rest)
+
+
 def solution(mesh):
     return jax.shard_map(
         body,

time: 642 us -> 286 us (0.45)
  local copies, waits for them, and re-layouts: 236 us -> 3.84 us
  other arithmetic: 83.2 us -> 0.86 us
  matrix products: 82.1 us -> 0 us
  Pallas kernels: 0 us -> 75.9 us
  waiting for transfers between devices: 212 us -> 192 us
  between operations: 13.6 us -> 0.14 us
    ppermute x0 -> x8, waiting for transfers between devices: none -> 192 us  [exchange(): return lax.ppermute(value, axis, [(i, i ^ bit) for i in range(count)])]
    all_to_all x2 -> x0, waiting for transfers between devices: 191 us -> none  [the longest x1 138 us: body(): lax.all_to_all(source_send, 'shot', split_axis=2, concat_axis=0, tiled=True)]
    gather x3 -> x0, local copies, waits for them, and re-layouts: 82.8 us -> none  [the longest x2 72.8 us: extrapolate(): jnp.take(wavefield, columns, axis=1)]
    dot_general x5 -> x0, matrix products: 82.1 us -> none  [the longest x1 32.3 us: data_product(): jnp.einsum('ncsr,nsk->ncrk', lax.all_gather(data_shard, 'shot', axis=0, t...]
    pallas_call x0 -> x7, Pallas kernels: none -> 75.9 us  [the longest x2 40.6 us: extrapolate_blocks(): pl.pallas_call(functools.partial(extrapolate_kernel, rows=rows, blocks=bl...]
    reshape x4 -> x0, local copies, waits for them, and re-layouts: 46.3 us -> none  [the longest x2 41.4 us: extrapolate(): jnp.take(wavefield, columns, axis=1)]
    concatenate x1 -> x0, local copies, waits for them, and re-layouts: 32.1 us -> none  [data_product(): contribution = jnp.concatenate([real_part, imag_part], -1)]
    select_n x1, other arithmetic: 26.5 us -> 0.01 us  [split_body(): (jnp.arange(blocks, dtype=jnp.int32)[:, None] + band_offsets) % blocks]
  transfers between devices with their start and end apart: 4 -> 8, of which waited for: 3 -> 4; matrix products, arithmetic and copies ran while one was open for 14% -> 0% of each run, Pallas kernels for 0% -> 18%
where the time goes in v1:
time: 286 us; the launch traced here: 285 us
  waiting for transfers between devices  192 us (67%)
  Pallas kernels  75.9 us (27%)
  starting transfers between devices  12.3 us (4%)
  local copies, waits for them, and re-layouts  3.84 us (1%)
    ppermute x8, waiting for transfers between devices, exchange(): return lax.ppermute(value, axis, [(i, i ^ bit) for i in range(count)])  192 us
    pallas_call x2, Pallas kernels, extrapolate_blocks(): pl.pallas_call(functools.partial(extrapolate_kernel, rows=rows, blocks=bl...  40.6 us
    pallas_call x4, Pallas kernels, image_blocks(): pl.pallas_call(functools.partial(kernel, size=size), grid_spec=pltpu.Pref...  21.5 us
    pallas_call x1, Pallas kernels, product_blocks(): pl.pallas_call(product_kernel, grid_spec=pltpu.PrefetchScalarGridSpec(num...  13.8 us
    ppermute x8, starting transfers between devices, exchange(): return lax.ppermute(value, axis, [(i, i ^ bit) for i in range(count)])  12.3 us
  transfers between devices with their start and end apart: 8, of which 4 were waited for; matrix products, arithmetic and copies ran while one was open for 0% of the time, Pallas kernels for 18%

profile of v1, /device:TPU:0, one launch (start us, length us, event | category | flops | bytes accessed | tf_op | source)
XLA Modules:
  0.0 285.4 jit_solution(1396138386723951942)
XLA Ops:
  0.0 0.8 copy.7
  0.8 0.1 pad_add_fusion.order
  0.9 20.0 %extrapolate.2 = (bf16[8,512,256]{2,1,0:T(8,128)(2,1)S(1)}, bf16[8,512,256]{2,1,0:T(8,128)(2,1)}) custom-call(s32[16]{0:T(128)S(1)} %pad_add_fusion.order, s32[16,3]{1,0:T(8,128)S(1)} %add_select_fusion.columns, bf16[16384,128]{1,0:T(8,128)(2,1)} %bitcast.31, bf16[16,3,2,128,128]{4,3,2,1,0:T(8,128)(2,1)} %bitcast.33), custom_call_target="tpu_custom_call" | custom-call | flops 3221225472 | bytes 16777216 | tf_op jit(solution)/shard_map/extrapolate/pallas_call | solution.py:154
  20.9 1.3 copy-done.1
  22.2 3.0 %collective-permute-start = (bf16[8,512,256]{2,1,0:T(8,128)(2,1)}, bf16[8,512,256]{2,1,0:T(8,128)(2,1)}, u32[]{:S(2)}, u32[]{:S(2)}) collective-permute-start(bf16[8,512,256]{2,1,0:T(8,128)(2,1)} %get-tuple-element.10), channel_id=1, source_target_pairs={{0,4},{4,0},{8,12},{12,8},{1,5},{5,1},{9,13},{13,9},{2,6},{6,2},{1... | collective-permute-start | bytes 6291464 | tf_op jit(solution)/shard_map/ppermute | solution.py:284
  25.2 20.5 %extrapolate.3 = (bf16[8,512,256]{2,1,0:T(8,128)(2,1)}, bf16[8,512,256]{2,1,0:T(8,128)(2,1)}) custom-call(s32[16]{0:T(128)S(1)} %pad_add_fusion.order, s32[16,3]{1,0:T(8,128)S(1)} %add_select_fusion.columns, bf16[16384,128]{1,0:T(8,128)(2,1)} %bitcast.32, bf16[16,3,2,128,128]{4,3,2,1,0:T(8,128)(2,1)} %bitcast.34), custom_call_target="tpu_custom_call" | custom-call | flops 3221225472 | bytes 16777216 | tf_op jit(solution)/shard_map/extrapolate/pallas_call | solution.py:154
  45.8 0.0 collective-permute-start.4
  45.8 3.0 %collective-permute-start.3 = (bf16[8,512,256]{2,1,0:T(8,128)(2,1)}, bf16[8,512,256]{2,1,0:T(8,128)(2,1)}, u32[]{:S(2)}, u32[]{:S(2)}) collective-permute-start(bf16[8,512,256]{2,1,0:T(8,128)(2,1)} %get-tuple-element.12.field), channel_id=1, source_target_pairs={{0,8},{4,12},{8,0},{12,4},{1,9},{5,13},{9,1},{13,5},{2,10},{6,14},... | collective-permute-start | bytes 6291464 | tf_op jit(solution)/shard_map/ppermute | solution.py:284
  48.8 1.3 collective-permute-start.2
  50.2 0.0 copy-done
  50.2 0.2 collective-permute-start.1
  50.4 0.0 copy-done.3
  50.4 0.1 fusion.4
  50.5 178.0 %collective-permute-done.1.far_data = bf16[16,2,128,128]{3,2,1,0:T(8,128)(2,1)} collective-permute-done((bf16[16,2,128,128]{3,2,1,0:T(8,128)(2,1)S(1)}, bf16[16,2,128,128]{3,2,1,0:T(8,128)(2,1)}, u32[]{:S(2)}, u32[]{:S(2)}) %collective-permute-start.1) | collective-permute-done | bytes 1048608 | tf_op jit(solution)/shard_map/ppermute | solution.py:284
  228.5 0.0 collective-permute-done.far
  228.5 1.6 copy-done.2
  230.1 13.8 %product.1 = bf16[8,256,2048]{2,1,0:T(8,128)(2,1)} custom-call(s32[16]{0:T(128)S(1)} %get-tuple-element.14.near_ids, s32[16]{0:T(128)S(1)} %get-tuple-element.13.far_ids, bf16[8,512,256]{2,1,0:T(8,128)(2,1)S(1)} %copy-done.2, bf16[8,512,256]{2,1,0:T(8,128)(2,1)} %collective-permute-done.far, bf16[16,2,128,128]{3,2,1,0:T(8,128)(2,1)S(1)} %bitcast.30, ...), custom_call_target="tpu_custom_call" | custom-call | flops 4294967296 | bytes 16777216 | tf_op jit(solution)/shard_map/product/pallas_call | solution.py:217
  243.9 5.5 %image.4.before = f32[8,2,128,128]{3,2,1,0:T(8,128)S(1)} custom-call(s32[1]{0:T(128)} %bitcast.9.origin, bf16[8,256,2048]{2,1,0:T(8,128)(2,1)} %product.1, bf16[8,512,256]{2,1,0:T(8,128)(2,1)} %get-tuple-element.12.field), custom_call_target="tpu_custom_call" | custom-call | flops 536870912 | bytes 6291456 | tf_op jit(solution)/shard_map/image/pallas_call | solution.py:266
  249.4 0.0 collective-permute-done.4.field
  249.4 5.5 %image.5.before = f32[8,2,128,128]{3,2,1,0:T(8,128)S(1)} custom-call(s32[1]{0:T(128)} %bitcast.8.origin, bf16[8,256,2048]{2,1,0:T(8,128)(2,1)} %product.1, bf16[8,512,256]{2,1,0:T(8,128)(2,1)} %collective-permute-done.4.field, f32[8,2,128,128]{3,2,1,0:T(8,128)S(1)} %image.4.before), custom_call_target="tpu_custom_call" | custom-call | flops 536870912 | bytes 6291456 | tf_op jit(solution)/shard_map/image/pallas_call | solution.py:266
  254.9 0.0 collective-permute-done.3.field
  254.9 5.5 %image.6.before = f32[8,2,128,128]{3,2,1,0:T(8,128)S(1)} custom-call(s32[1]{0:T(128)} %bitcast.7.origin, bf16[8,256,2048]{2,1,0:T(8,128)(2,1)} %product.1, bf16[8,512,256]{2,1,0:T(8,128)(2,1)} %collective-permute-done.3.field, f32[8,2,128,128]{3,2,1,0:T(8,128)S(1)} %image.5.before), custom_call_target="tpu_custom_call" | custom-call | flops 536870912 | bytes 6291456 | tf_op jit(solution)/shard_map/image/pallas_call | solution.py:266
  260.4 0.0 collective-permute-done.2.field
  260.4 5.1 %image.7 = f32[8,2,128,128]{3,2,1,0:T(8,128)S(1)} custom-call(s32[1]{0:T(128)} %bitcast.origin, bf16[8,256,2048]{2,1,0:T(8,128)(2,1)} %product.1, bf16[8,512,256]{2,1,0:T(8,128)(2,1)S(1)} %collective-permute-done.2.field, f32[8,2,128,128]{3,2,1,0:T(8,128)S(1)} %image.6.before), custom_call_target="tpu_custom_call" | custom-call | flops 536870912 | bytes 6291456 | tf_op jit(solution)/shard_map/image/pallas_call | solution.py:266
  265.5 0.1 collective-permute-start.5
  265.6 1.9 collective-permute-done.5
  267.5 0.1 bitcast_add_fusion
  267.6 1.7 collective-permute-start.6
  269.3 6.7 %collective-permute-done.6 = f32[2,2,128,128]{3,2,1,0:T(8,128)S(1)} collective-permute-done((f32[2,2,128,128]{3,2,1,0:T(8,128)S(1)}, f32[2,2,128,128]{3,2,1,0:T(8,128)S(1)}, u32[]{:S(2)}, u32[]{:S(2)}) %collective-permute-start.6) | collective-permute-done | bytes 262176 | tf_op jit(solution)/shard_map/ppermute | solution.py:284
  276.0 2.9 %collective-permute-start.7 = (f32[2,128,128]{2,1,0:T(8,128)S(1)}, f32[2,128,128]{2,1,0:T(8,128)S(1)}, u32[]{:S(2)}, u32[]{:S(2)}) collective-permute-start(f32[2,128,128]{2,1,0:T(8,128)S(1)} %dynamic-slice_bitcast_fusion.2), channel_id=1, source_target_pairs={{0,8},{4,12},{8,0},{12,4},{1,9},{5,13},{9,1},{13,5},{2,10},{6,14},... | collective-permute-start | bytes 393224 | tf_op jit(solution)/shard_map/ppermute | solution.py:284
  279.0 5.8 %collective-permute-done.7 = f32[2,128,128]{2,1,0:T(8,128)S(1)} collective-permute-done((f32[2,128,128]{2,1,0:T(8,128)S(1)}, f32[2,128,128]{2,1,0:T(8,128)S(1)}, u32[]{:S(2)}, u32[]{:S(2)}) %collective-permute-start.7) | collective-permute-done | bytes 131104 | tf_op jit(solution)/shard_map/ppermute | solution.py:284
  284.7 0.7 fusion
  (11 shorter events, 0.2 us)
Async XLA Ops:
  20.9 1.3 copy-start.1
  22.2 206.3 %collective-permute-start = (bf16[8,512,256]{2,1,0:T(8,128)(2,1)}, bf16[8,512,256]{2,1,0:T(8,128)(2,1)}, u32[]{:S(2)}, u32[]{:S(2)}) collective-permute-start(bf16[8,512,256]{2,1,0:T(8,128)(2,1)} %get-tuple-element.10), channel_id=1, source_target_pairs={{0,4},{4,0},{8,12},{12,8},{1,5},{5,1},{9,13},{13,9},{2,6},{6,2},{1... | collective-permute-start | bytes 6291464 | tf_op jit(solution)/shard_map/ppermute | solution.py:284
  25.2 24.9 %copy-start = (bf16[1,16,2,128,128]{4,3,2,1,0:T(8,128)(2,1)S(1)}, bf16[1,16,2,128,128]{4,3,2,1,0:T(8,128)(2,1)}, u32[]{:S(2)}) copy-start(bf16[1,16,2,128,128]{4,3,2,1,0:T(8,128)(2,1)} %param.11) | copy-start | bytes 3145732
  25.2 25.2 %copy-start.3 = (s32[64,2]{0,1:T(2,128)S(1)}, s32[64,2]{0,1:T(2,128)}, u32[]{:S(2)}) copy-start(s32[64,2]{0,1:T(2,128)} %param.10) | copy-start | bytes 1540
  45.8 203.6 %collective-permute-start.4 = (bf16[8,512,256]{2,1,0:T(8,128)(2,1)}, bf16[8,512,256]{2,1,0:T(8,128)(2,1)}, u32[]{:S(2)}, u32[]{:S(2)}) collective-permute-start(bf16[8,512,256]{2,1,0:T(8,128)(2,1)} %get-tuple-element.11), channel_id=1, source_target_pairs={{0,4},{4,0},{8,12},{12,8},{1,5},{5,1},{9,13},{13,9},{2,6},{6,2},{1... | collective-permute-start | bytes 6291464 | tf_op jit(solution)/shard_map/ppermute | solution.py:284
  45.8 209.1 %collective-permute-start.3 = (bf16[8,512,256]{2,1,0:T(8,128)(2,1)}, bf16[8,512,256]{2,1,0:T(8,128)(2,1)}, u32[]{:S(2)}, u32[]{:S(2)}) collective-permute-start(bf16[8,512,256]{2,1,0:T(8,128)(2,1)} %get-tuple-element.12.field), channel_id=1, source_target_pairs={{0,8},{4,12},{8,0},{12,4},{1,9},{5,13},{9,1},{13,5},{2,10},{6,14},... | collective-permute-start | bytes 6291464 | tf_op jit(solution)/shard_map/ppermute | solution.py:284
  48.8 211.5 %collective-permute-start.2 = (bf16[8,512,256]{2,1,0:T(8,128)(2,1)}, bf16[8,512,256]{2,1,0:T(8,128)(2,1)S(1)}, u32[]{:S(2)}, u32[]{:S(2)}) collective-permute-start(bf16[8,512,256]{2,1,0:T(8,128)(2,1)} %get-tuple-element.11), channel_id=1, source_target_pairs={{0,12},{4,8},{8,4},{12,0},{1,13},{5,9},{9,5},{13,1},{2,14},{6,10},... | collective-permute-start | bytes 6291464 | tf_op jit(solution)/shard_map/ppermute | solution.py:284
  50.2 178.3 %collective-permute-start.1 = (bf16[16,2,128,128]{3,2,1,0:T(8,128)(2,1)S(1)}, bf16[16,2,128,128]{3,2,1,0:T(8,128)(2,1)}, u32[]{:S(2)}, u32[]{:S(2)}) collective-permute-start(bf16[16,2,128,128]{3,2,1,0:T(8,128)(2,1)S(1)} %bitcast.29), channel_id=1, source_target_pairs={{0,4},{4,0},{8,12},{12,8},{1,5},{5,1},{9,13},{13,9},{2,6},{6,2},{1... | collective-permute-start | bytes 3145736 | tf_op jit(solution)/shard_map/ppermute | solution.py:284
  228.5 1.6 copy-start.2
  265.5 2.0 collective-permute-start.5
  267.6 8.4 %collective-permute-start.6 = (f32[2,2,128,128]{3,2,1,0:T(8,128)S(1)}, f32[2,2,128,128]{3,2,1,0:T(8,128)S(1)}, u32[]{:S(2)}, u32[]{:S(2)}) collective-permute-start(f32[2,2,128,128]{3,2,1,0:T(8,128)S(1)} %dynamic-slice_bitcast_fusion.1), channel_id=1, source_target_pairs={{0,2},{1,3},{2,0},{3,1},{4,6},{5,7},{6,4},{7,5},{8,10},{9,11},{10,... | collective-permute-start | bytes 786440 | tf_op jit(solution)/shard_map/ppermute | solution.py:284
  276.0 8.7 %collective-permute-start.7 = (f32[2,128,128]{2,1,0:T(8,128)S(1)}, f32[2,128,128]{2,1,0:T(8,128)S(1)}, u32[]{:S(2)}, u32[]{:S(2)}) collective-permute-start(f32[2,128,128]{2,1,0:T(8,128)S(1)} %dynamic-slice_bitcast_fusion.2), channel_id=1, source_target_pairs={{0,8},{4,12},{8,0},{12,4},{1,9},{5,13},{9,1},{13,5},{2,10},{6,14},... | collective-permute-start | bytes 393224 | tf_op jit(solution)/shard_map/ppermute | solution.py:284
